TPU v7x, 512 devices: a whole 4x8x8 slice. The times are simulated.
512 devices in a mesh: row: 16 (over y_lo, x, core), col: 32 (over y_hi, z).
Axes of the slice: x: 4, y: 8 (y_hi: 4, y_lo: 2; y = y_hi * 2 + y_lo), z: 8, core: 2. Of those that a mesh axis runs over, the one named last changes fastest.
Arguments:
- inputs: bfloat16 [512, 12288], P('col', 'row'), may hold values from -6 to 6
- w_in: bfloat16 [12288, 24576], P('row', 'col'), may hold values from -0.0546875 to 0.0546875
- w_out: bfloat16 [24576, 12288], P('col', 'row'), may hold values from -0.0390625 to 0.0390625
- out_grad: bfloat16 [512, 12288], P('col', 'row'), may hold values from -6 to 6
Outputs:
- grad_inputs: bfloat16 [512, 12288], P('col', 'row')
- grad_w_in: bfloat16 [12288, 24576], P('row', 'col')
- grad_w_out: bfloat16 [24576, 12288], P('col', 'row')
All inputs are finite; a program needn't handle non-finite values.
Results may differ from a plain program's by a relative error of at most 0.005.
Values may be sent and summed in bfloat16 or wider, within the bound.
A program may use at most 64 MiB of HBM per device.

v0:
```python
import math

import jax
import jax.numpy as jnp
from jax import lax
from jax.sharding import PartitionSpec as P

gelu_c = math.sqrt(2.0 / math.pi)


def gelu_parts(pre):
    inner = gelu_c * (pre + 0.044715 * pre * pre * pre)
    tanh_v = jnp.tanh(inner)
    value = 0.5 * pre * (1.0 + tanh_v)
    slope = 0.5 * (1.0 + tanh_v) + 0.5 * pre * (1.0 - tanh_v * tanh_v) * gelu_c * (
        1.0 + 3.0 * 0.044715 * pre * pre
    )
    return (value, slope)


def activate(pre, hidden_grad):
    value, slope = gelu_parts(pre)
    return (value.astype(jnp.bfloat16), (slope * hidden_grad).astype(jnp.bfloat16))


def local(inputs, w_in, w_out, out_grad):
    all_inputs = lax.all_gather(inputs, "col", axis=0, tiled=True)
    all_grads = lax.all_gather(out_grad, "col", axis=0, tiled=True)
    pre_part = jnp.dot(all_inputs, w_in, preferred_element_type=jnp.float32)
    grad_part = lax.dot_general(
        all_grads, w_out, (((1,), (1,)), ((), ())), preferred_element_type=jnp.float32
    )
    pre, hidden_grad = lax.psum((pre_part, grad_part), "row")
    hidden, pre_grad = activate(pre, hidden_grad)
    grad_w_out = lax.dot_general(
        hidden, all_grads, (((0,), (0,)), ((), ())), preferred_element_type=jnp.float32
    ).astype(jnp.bfloat16)
    grad_w_in = lax.dot_general(
        all_inputs, pre_grad, (((0,), (0,)), ((), ())), preferred_element_type=jnp.float32
    ).astype(jnp.bfloat16)
    grad_inputs = lax.psum_scatter(
        lax.dot_general(
            pre_grad, w_in, (((1,), (1,)), ((), ())), preferred_element_type=jnp.float32
        ),
        "col",
        scatter_dimension=0,
        tiled=True,
    ).astype(jnp.bfloat16)
    return (grad_inputs, grad_w_in, grad_w_out)


def solution(mesh):
    return jax.shard_map(
        local,
        mesh=mesh,
        in_specs=(P("col", "row"), P("row", "col"), P("col", "row"), P("col", "row")),
        out_specs=(P("col", "row"), P("row", "col"), P("col", "row")),
        check_vma=False,
    )
```

profile of v0, /device:TPU:1, one launch (start us, length us, event | category | flops | bytes accessed | tf_op | source)
XLA Modules:
  0.0 553.5 jit_solution(5214028974998073880)
XLA Ops:
  7.2 0.0 copy-start
  7.2 0.0 all-reduce.3.cloned.1.call-start
  7.2 0.0 copy-start.2
  7.2 80.5 %all_gather.6 = bf16[512,768]{1,0:T(8,128)(2,1)S(1)} all-gather(bf16[16,768]{1,0:T(8,128)(2,1)} %param.4), channel_id=1, replica_groups=mesh['row'=16,'col'=32] {'col'}, dimensions={0}, use_global_device_ids=true | all-gather | bytes 811008 | tf_op jit(solution)/shard_map/all_gather | solution.py:27
  87.7 67.3 %all_gather.7 = bf16[512,768]{1,0:T(8,128)(2,1)S(1)} all-gather(bf16[16,768]{1,0:T(8,128)(2,1)} %param.7), channel_id=1, replica_groups=mesh['row'=16,'col'=32] {'col'}, dimensions={0}, use_global_device_ids=true | all-gather | bytes 811008 | tf_op jit(solution)/shard_map/all_gather | solution.py:28
  155.0 0.0 copy-done.2
  155.0 2.0 fusion.17
  156.9 0.0 copy-done
  156.9 1.9 fusion.16
  158.9 0.0 all-reduce.3.cloned.1.call-update
  158.9 0.0 reduce-scatter.2.cloned.1.call-start
  159.0 157.3 %all-reduce.3.cloned.1.call-done = (f32[512,768]{1,0:T(8,128)}, f32[512,768]{1,0:T(8,128)}) async-done(((f32[512,768]{1,0:T(8,128)}, f32[512,768]{1,0:T(8,128)}), (f32[512,768]{1,0:T(8,128)}, f32[512,768]{1,0:T(8,128)})) %all-reduce.3.cloned.1.call-update) | async-done | bytes 3145744 | tf_op jit(solution)/shard_map/psum | solution.py:33
  316.2 2.9 fusion.6
  319.1 2.0 fusion.18
  321.0 0.0 reduce-scatter.2.cloned.1.call-update
  321.1 1.8 fusion.7
  322.9 0.0 copy-start.1
  322.9 2.5 copy.7
  325.4 0.0 copy-done.1
  325.4 2.0 convolution_convert_fusion
  327.4 217.9 %reduce-scatter.2.cloned.1.call-done = f32[16,768]{1,0:T(8,128)} async-done(((f32[512,768]{1,0:T(8,128)}), f32[16,768]{1,0:T(8,128)}) %reduce-scatter.2.cloned.1.call-update) | async-done | bytes 49168 | tf_op jit(solution)/shard_map/reduce_scatter | solution.py:41
  545.3 1.4 convert_element_type.19
Async XLA Ops:
  7.2 149.8 %copy-start = (bf16[768,768]{1,0:T(8,128)(2,1)S(1)}, bf16[768,768]{1,0:T(8,128)(2,1)}, u32[]{:S(2)}) copy-start(bf16[768,768]{1,0:T(8,128)(2,1)} %param.5) | copy-start | bytes 3538948
  7.2 309.0 %all-reduce.3.cloned.1.call-start = ((), (), s32[]{:S(2)}) async-start(), calls=%async_computation.2 | async-start | bytes 6291456 | tf_op jit(solution)/shard_map/psum | solution.py:33
  7.2 147.7 %copy-start.2 = (bf16[768,768]{1,0:T(8,128)(2,1)S(1)}, bf16[768,768]{1,0:T(8,128)(2,1)}, u32[]{:S(2)}) copy-start(bf16[768,768]{1,0:T(8,128)(2,1)} %param.6) | copy-start | bytes 3538948
  158.9 386.4 %reduce-scatter.2.cloned.1.call-start = ((), (), s32[]{:S(2)}) async-start(), calls=%async_computation.1 | async-start | bytes 1622016 | tf_op jit(solution)/shard_map/reduce_scatter | solution.py:41
  322.9 2.5 copy-start.1
Sparse Core Ops, SparseCore 0:
  159.0 157.1 all-reduce.2
  321.2 224.0 reduce-scatter.1
where the time goes:
time: 557 us; the launch traced here: 554 us
  waiting for transfers between devices  375 us (67%)
  blocking collectives  148 us (27%)
  between operations  14.1 us (3%)
  matrix products  9.66 us (2%)
    reduce_scatter x1, waiting for transfers between devices, local(): lax.psum_scatter(lax.dot_general(pre_grad, w_in, (((1,), (1,)), ((), ()))...  218 us
    psum x1, waiting for transfers between devices, local(): pre, hidden_grad = lax.psum((pre_part, grad_part), 'row')  157 us
    all_gather x1, blocking collectives, local(): all_inputs = lax.all_gather(inputs, 'col', axis=0, tiled=True)  80.5 us
    all_gather x1, blocking collectives, local(): all_grads = lax.all_gather(out_grad, 'col', axis=0, tiled=True)  67.3 us
  transfers between devices with their start and end apart: 2, of which 2 were waited for; matrix products, arithmetic and copies ran while one was open for 1% of the time, Pallas kernels for 0%

commit v1 on v0

v1 whole, which is shorter than its diff:
```python
import math

import jax
import jax.numpy as jnp
from jax import lax
from jax.experimental import pallas as pl
from jax.experimental.pallas import tpu as pltpu
from jax.sharding import PartitionSpec as P

MESH = pl.DeviceIdType.MESH
BF16, F32 = jnp.bfloat16, jnp.float32
GELU_C = math.sqrt(2.0 / math.pi)

NZ, NYH, NX, NYL = 8, 4, 4, 2
NQ = NX * NYL
TOK = 16
BLK = NYH * TOK
CH = 2 * BLK
NCH = 4
POS = {0: 0, 1: 1, 7: 2, 2: 3, 6: 4, 3: 5, 5: 6, 4: 7}
DIST = {p: d for d, p in POS.items()}
HOPS = [(dx, dy) for dy in range(NYL) for dx in range(NX) if (dx, dy) != (0, 0)]


def activate(pre, hidden_grad):
    inner = GELU_C * (pre + 0.044715 * pre * pre * pre)
    t = jnp.tanh(inner)
    value = 0.5 * pre * (1.0 + t)
    slope = 0.5 * (1.0 + t) + 0.5 * pre * (1.0 - t * t) * GELU_C * (
        1.0 + 3.0 * 0.044715 * pre * pre
    )
    return value.astype(BF16), (slope * hidden_grad).astype(BF16)


def kernel(
    x_hbm, win_hbm, wout_hbm, og_hbm,
    gi_ref, gwin_hbm, gwout_hbm,
    act, win, wout, part, crecv, sendb, own32, rrecv, agall, hid, pg,
    g0, gsend, grecv, ysend, yrecv, gw,
    lsem, ssem, agsem, csem, rsem, zsem, ysem,
):
    row, col = lax.axis_index("row"), lax.axis_index("col")
    core = lax.rem(row, 2)
    x = lax.rem(lax.div(row, 2), NX)
    ylo = lax.div(row, 2 * NX)
    yhi, z = lax.div(col, NZ), lax.rem(col, NZ)
    q = ylo * NX + x
    ncol = win.shape[1]
    half = ncol // NYL

    def at(dx=0, dy=0, dc=0, e=0, d=0):
        r = lax.rem(ylo + dy, NYL) * (2 * NX) + lax.rem(x + dx, NX) * 2 + lax.rem(core + dc, 2)
        c = lax.rem(yhi + e, NYH) * NZ + lax.rem(z + d, NZ)
        return (r, c)

    def chip(dx, dy):
        return lax.rem(ylo + dy, NYL) * NX + lax.rem(x + dx, NX)

    loads = [
        pltpu.make_async_copy(x_hbm, act.at[0, pl.ds(0, TOK)], lsem.at[0]),
        pltpu.make_async_copy(og_hbm, act.at[1, pl.ds(0, TOK)], lsem.at[1]),
        pltpu.make_async_copy(win_hbm, win, lsem.at[2]),
        pltpu.make_async_copy(wout_hbm, wout, lsem.at[3]),
    ]
    for c in loads:
        c.start()
    peers = (
        [at(dc=1)]
        + [at(dx=dx, dy=dy) for dx, dy in HOPS]
        + [at(e=e) for e in range(1, NYH)]
        + [at(d=d) for d in range(1, NZ)]
    )
    barrier = pltpu.get_barrier_semaphore()
    for p in peers:
        pl.semaphore_signal(barrier, inc=1, device_id=p, device_id_type=MESH)
    pl.semaphore_wait(barrier, len(peers))
    loads[0].wait()
    loads[1].wait()

    sent = []

    def send(src, dst, recv_sem, device):
        c = pltpu.make_async_remote_copy(
            src_ref=src, dst_ref=dst, send_sem=ssem.at[len(sent)], recv_sem=recv_sem,
            device_id=device, device_id_type=MESH,
        )
        c.start()
        sent.append(c)

    def arrived(ref, sem):
        pltpu.make_async_copy(ref, ref, sem).wait()

    def piece(d, e):
        return act.at[:, pl.ds(POS[d] * BLK + e * TOK, TOK)]

    def half_piece(a, d, e):
        return act.at[a, pl.ds(POS[d] * BLK + e * TOK, TOK)]

    down, up = at(d=NZ - 1), at(d=1)

    def forward(d, e):
        if d < 3:
            send(piece(d, e), piece(d + 1, e), agsem.at[POS[d + 1], e], down)
        if d == 3:
            send(half_piece(0, 3, e), half_piece(0, 4, e), agsem.at[POS[4], e], down)
        if d == 0 or d > 5:
            to = (d - 1) % NZ
            send(piece(d, e), piece(to, e), agsem.at[POS[to], e], up)
        if d == 5:
            send(half_piece(1, 5, e), half_piece(1, 4, e), agsem.at[NZ, e], up)

    def take(d, e):
        if d == 4:
            arrived(half_piece(0, 4, e), agsem.at[POS[4], e])
            arrived(half_piece(1, 4, e), agsem.at[NZ, e])
        else:
            arrived(piece(d, e), agsem.at[POS[d], e])
            forward(d, e)

    def take_ring(i, e):
        take(i, e)
        take(NZ - i, e)

    def multiply(ci):
        rows = pl.ds(ci * CH, CH)
        pre = jnp.dot(act[0, rows], win[...], preferred_element_type=F32)
        part[ci, 0, 0] = pre[:BLK]
        part[ci, 1, 0] = pre[BLK:]
        hg = lax.dot_general(
            act[1, rows], wout[...], (((1,), (1,)), ((), ())), preferred_element_type=F32
        )
        part[ci, 0, 1] = hg[:BLK]
        part[ci, 1, 1] = hg[BLK:]
        send(part.at[ci, 1 - core], crecv.at[ci], csem.at[0, ci], at(dc=1))

    def scatter(ci):
        arrived(crecv.at[ci], csem.at[0, ci])
        for k in range(NQ):
            r, c = pl.ds((k % NX) * TOK, TOK), pl.ds((k // NX) * half, half)
            total = part[ci, core, :, r, c] + crecv[ci, :, r, c]
            own32[ci, k] = total
            sendb[ci, k] = total.astype(BF16)
        for k, (dx, dy) in enumerate(HOPS):
            send(sendb.at[ci, chip(dx, dy)], rrecv.at[ci, k], rsem.at[0, ci], at(dx=dx, dy=dy))

    def activation(ci):
        arrived(rrecv.at[ci], rsem.at[0, ci])
        total = own32[ci, q]
        for k in range(NQ - 1):
            total = total + rrecv[ci, k].astype(F32)
        value, slope = activate(total[0], total[1])
        agall[ci, core, q, 0] = value
        agall[ci, core, q, 1] = slope
        for dx, dy in HOPS:
            send(agall.at[ci, core, q], agall.at[ci, core, q], rsem.at[1, ci], at(dx=dx, dy=dy))

    def share(ci):
        arrived(rrecv.at[ci], rsem.at[1, ci])
        send(agall.at[ci, core], agall.at[ci, core], csem.at[1, ci], at(dc=1))

    def back(ci):
        arrived(agall.at[ci, 0], csem.at[1, ci])
        for h in range(2):
            for k in range(NQ):
                r = pl.ds(ci * CH + h * BLK + (k % NX) * TOK, TOK)
                c = pl.ds((k // NX) * half, half)
                hid[r, c] = agall[ci, h, k, 0]
                pg[r, c] = agall[ci, h, k, 1]
        g = lax.dot_general(
            pg[pl.ds(ci * CH, CH)], win[...], (((1,), (1,)), ((), ())), preferred_element_type=F32
        )
        for h in range(2):
            d = DIST[2 * ci + h]
            block = g[h * BLK:(h + 1) * BLK]
            if d == 0:
                g0[...] = block
            else:
                gsend[d] = block.astype(BF16)
                send(gsend.at[d], grecv.at[d], zsem.at[d], at(d=d))

    def weight_grads():
        out = []
        for a, (lhs, rhs, dst) in enumerate(
            ((hid, act.at[1], gwout_hbm), (act.at[0], pg, gwin_hbm))
        ):
            step = 256
            for i in range(lhs.shape[1] // step):
                r = pl.ds(i * step, step)
                gw[a, r] = lax.dot_general(
                    lhs[:, r], rhs[...], (((0,), (0,)), ((), ())), preferred_element_type=F32
                ).astype(BF16)
                c = pltpu.make_async_copy(gw.at[a, r], dst.at[r], lsem.at[4 + a * 3 + i])
                c.start()
                out.append(c)
        return out

    forward(0, 0)
    for e in (1, 3, 2):
        send(piece(0, 0), piece(0, e), agsem.at[0, e], at(e=NYH - e))
    for e in (1, 3):
        take(0, e)
    take_ring(1, 0)
    take(0, 2)
    for e in (1, 3):
        take_ring(1, e)
    take_ring(2, 0)
    take_ring(1, 2)
    loads[2].wait()
    loads[3].wait()
    multiply(0)
    for e in (1, 3):
        take_ring(2, e)
    scatter(0)
    take_ring(3, 0)
    take_ring(2, 2)
    multiply(1)
    for e in (1, 3):
        take_ring(3, e)
    scatter(1)
    take_ring(3, 2)
    multiply(2)
    activation(0)
    scatter(2)
    for e in (0, 1, 3, 2):
        take(4, e)
    multiply(3)
    activation(1)
    scatter(3)
    share(0)
    activation(2)
    back(0)
    share(1)
    activation(3)
    back(1)
    share(2)
    back(2)
    share(3)
    back(3)
    stores = weight_grads()
    total = g0[...]
    for d in range(1, NZ):
        arrived(grecv.at[d], zsem.at[d])
        total = total + grecv[d].astype(F32)
    for e in range(NYH):
        ysend[e] = total[e * TOK:(e + 1) * TOK]
    for e in range(1, NYH):
        send(ysend.at[e], yrecv.at[e], ysem.at[e], at(e=e))
    total = ysend[0]
    for e in range(1, NYH):
        arrived(yrecv.at[e], ysem.at[e])
        total = total + yrecv[e]
    gi_ref[...] = total.astype(BF16)
    for c in sent:
        c.wait_send()
    for c in stores:
        c.wait()


N_SENDS = 32 + 3 + 2 * NCH + 2 * 7 * NCH + (NZ - 1) + (NYH - 1)


def local(inputs, w_in, w_out, out_grad):
    feat, ff = w_in.shape
    half = ff // NYL
    tokens = TOK * NYH * NZ
    any_spec = pl.BlockSpec(memory_space=pl.ANY)
    vmem = pltpu.VMEM
    return pl.pallas_call(
        kernel,
        out_shape=(
            jax.ShapeDtypeStruct(inputs.shape, BF16),
            jax.ShapeDtypeStruct(w_in.shape, BF16),
            jax.ShapeDtypeStruct(w_out.shape, BF16),
        ),
        in_specs=[any_spec] * 4,
        out_specs=(pl.BlockSpec(memory_space=pltpu.VMEM), any_spec, any_spec),
        scratch_shapes=[
            vmem((2, tokens, feat), BF16),
            vmem((feat, ff), BF16),
            vmem((ff, feat), BF16),
            vmem((NCH, 2, 2, BLK, ff), F32),
            vmem((NCH, 2, BLK, ff), F32),
            vmem((NCH, NQ, 2, TOK, half), BF16),
            vmem((NCH, NQ, 2, TOK, half), F32),
            vmem((NCH, NQ - 1, 2, TOK, half), BF16),
            vmem((NCH, 2, NQ, 2, TOK, half), BF16),
            vmem((tokens, ff), BF16),
            vmem((tokens, ff), BF16),
            vmem((BLK, feat), F32),
            vmem((NZ, BLK, feat), BF16),
            vmem((NZ, BLK, feat), BF16),
            vmem((NYH, TOK, feat), F32),
            vmem((NYH, TOK, feat), F32),
            vmem((2, feat, ff), BF16),
            pltpu.SemaphoreType.DMA((10,)),
            pltpu.SemaphoreType.DMA((N_SENDS,)),
            pltpu.SemaphoreType.DMA((NZ + 1, NYH)),
            pltpu.SemaphoreType.DMA((2, NCH)),
            pltpu.SemaphoreType.DMA((2, NCH)),
            pltpu.SemaphoreType.DMA((NZ,)),
            pltpu.SemaphoreType.DMA((NYH,)),
        ],
        compiler_params=pltpu.CompilerParams(
            collective_id=0, has_side_effects=True, vmem_limit_bytes=48 * 2**20
        ),
        cost_estimate=pl.CostEstimate(
            flops=10 * tokens * feat * ff, bytes_accessed=8 * feat * ff, transcendentals=0
        ),
    )(inputs, w_in, w_out, out_grad)


def solution(mesh):
    return jax.shard_map(
        local,
        mesh=mesh,
        in_specs=(P("col", "row"), P("row", "col"), P("col", "row"), P("col", "row")),
        out_specs=(P("col", "row"), P("row", "col"), P("col", "row")),
        check_vma=False,
    )
```

time: 557 us -> 85.1 us (0.15)
  waiting for transfers between devices: 375 us -> 0 us
  blocking collectives: 148 us -> 0 us
  Pallas kernels: 0 us -> 77.4 us
  between operations: 14.1 us -> 0.65 us
  matrix products: 9.66 us -> 0 us
    reduce_scatter x1 -> x0, waiting for transfers between devices: 218 us -> none  [local(): lax.psum_scatter(lax.dot_general(pre_grad, w_in, (((1,), (1,)), ((), ()))...]
    psum x1 -> x0, waiting for transfers between devices: 157 us -> none  [local(): pre, hidden_grad = lax.psum((pre_part, grad_part), 'row')]
    all_gather x2 -> x0, blocking collectives: 148 us -> none  [the longest x1 80.5 us: local(): all_inputs = lax.all_gather(inputs, 'col', axis=0, tiled=True)]
    pallas_call x0 -> x1, Pallas kernels: none -> 77.4 us  [local(): pl.pallas_call(kernel, out_shape=(jax.ShapeDtypeStruct(inputs.shape, BF16...]
    dot_general x5 -> x0, matrix products: 9.66 us -> none  [the longest x1 1.97 us: local(): lax.dot_general(all_grads, w_out, (((1,), (1,)), ((), ())), preferred_ele...]
  transfers between devices with their start and end apart: 2 -> 0, of which waited for: 2 -> 0; matrix products, arithmetic and copies ran while one was open for 1% -> 0% of each run, Pallas kernels for 0% -> 0%
where the time goes in v1:
time: 85.1 us; the launch traced here: 84.7 us
  Pallas kernels  77.4 us (91%)
  local copies, waits for them, and re-layouts  6.64 us (8%)
    pallas_call x1, Pallas kernels, local(): pl.pallas_call(kernel, out_shape=(jax.ShapeDtypeStruct(inputs.shape, BF16...  77.4 us
    unnamed x11, local copies, waits for them, and re-layouts  6.64 us

profile of v1, /device:TPU:1, one launch (start us, length us, event | category | flops | bytes accessed | tf_op | source)
XLA Modules:
  0.0 84.7 jit_solution(10661521445362251878)
XLA Ops:
  0.6 0.0 copy-start
  0.6 1.3 %copy-done = bf16[768,768]{1,0:T(8,128)(2,1)S(1)} copy-done((bf16[768,768]{1,0:T(8,128)(2,1)S(1)}, bf16[768,768]{1,0:T(8,128)(2,1)}, u32[]{:S(2)}) %copy-start) | copy-done | bytes 1179672
  1.9 0.0 copy-start.1
  1.9 1.3 %copy-done.1 = bf16[768,768]{1,0:T(8,128)(2,1)S(1)} copy-done((bf16[768,768]{1,0:T(8,128)(2,1)S(1)}, bf16[768,768]{1,0:T(8,128)(2,1)}, u32[]{:S(2)}) %copy-start.1) | copy-done | bytes 1179672
  3.2 0.0 copy-start.2
  3.2 0.7 copy-done.2
  3.9 0.0 copy-start.3
  3.9 0.7 copy-done.3
  4.6 77.4 %shard_map.67 = (bf16[16,768]{1,0:T(8,128)(2,1)S(1)}, bf16[768,768]{1,0:T(8,128)(2,1)S(1)}, bf16[768,768]{1,0:T(8,128)(2,1)S(1)}) custom-call(bf16[16,768]{1,0:T(8,128)(2,1)S(1)} %copy-done.2, bf16[768,768]{1,0:T(8,128)(2,1)S(1)} %copy-done, bf16[768,768]{1,0:T(8,128)(2,1)S(1)} %copy-done.1, bf16[16,768]{1,0:T(8,128)(2,1)S(1)} %copy-done.3), custom_call_target="tpu_custom_call" | custom-call | flops 3019898880 | bytes 4718592 | tf_op jit(solution)/shard_map/pallas_call | solution.py:268
  82.1 0.6 copy.10
  82.7 1.0 %copy.11 = bf16[768,768]{1,0:T(8,128)(2,1)} copy(bf16[768,768]{1,0:T(8,128)(2,1)S(1)} %get-tuple-element.7) | data formatting | bytes 2359296
  83.7 1.0 %copy.12 = bf16[768,768]{1,0:T(8,128)(2,1)} copy(bf16[768,768]{1,0:T(8,128)(2,1)S(1)} %get-tuple-element.8) | data formatting | bytes 2359296
Async XLA Ops:
  0.6 1.3 %copy-start = (bf16[768,768]{1,0:T(8,128)(2,1)S(1)}, bf16[768,768]{1,0:T(8,128)(2,1)}, u32[]{:S(2)}) copy-start(bf16[768,768]{1,0:T(8,128)(2,1)} %win_hbm.1) | copy-start | bytes 3538948
  1.9 1.3 %copy-start.1 = (bf16[768,768]{1,0:T(8,128)(2,1)S(1)}, bf16[768,768]{1,0:T(8,128)(2,1)}, u32[]{:S(2)}) copy-start(bf16[768,768]{1,0:T(8,128)(2,1)} %wout_hbm.1) | copy-start | bytes 3538948
  3.2 0.7 copy-start.2
  3.9 0.7 copy-start.3

commit v2 on v1

--- a/solution.py
+++ b/solution.py
@@ -17,9 +17,23 @@
 BLK = NYH * TOK
 CH = 2 * BLK
 NCH = 4
+TILE = 256
 POS = {0: 0, 1: 1, 7: 2, 2: 3, 6: 4, 3: 5, 5: 6, 4: 7}
 DIST = {p: d for d, p in POS.items()}
+NEAR, FAR = (1, 7, 2, 6), (3, 5, 4)
 HOPS = [(dx, dy) for dy in range(NYL) for dx in range(NX) if (dx, dy) != (0, 0)]
+
+ORDER = [
+    ("start",), ("ring", 1, 0), ("take", 0, 1), ("take", 0, 3), ("ring", 2, 0), ("take", 0, 2),
+    ("ring", 1, 1), ("ring", 1, 3), ("ring", 3, 0), ("ring", 1, 2),
+    ("weights",), ("mul", 0), ("ring", 2, 1), ("ring", 2, 3), ("scatter", 0),
+    ("ring", 2, 2), ("mul", 1), ("ring", 3, 1), ("ring", 3, 3), ("scatter", 1),
+    ("take", 4, 0), ("ring", 3, 2), ("mul", 2), ("act", 0), ("scatter", 2),
+    ("take", 4, 1), ("take", 4, 3), ("take", 4, 2), ("mul", 3), ("act", 1), ("scatter", 3),
+    ("share", 0), ("act", 2), ("back", 0), ("share", 1), ("act", 3), ("back", 1),
+    ("share", 2), ("back", 2), ("share", 3), ("back", 3), ("far", 3), ("grads", 0), ("near",),
+    ("far", 5), ("far", 4), ("grads", 1), ("end",),
+]
 
 
 def activate(pre, hidden_grad):
@@ -36,8 +50,8 @@
     x_hbm, win_hbm, wout_hbm, og_hbm,
     gi_ref, gwin_hbm, gwout_hbm,
     act, win, wout, part, crecv, sendb, own32, rrecv, agall, hid, pg,
-    g0, gsend, grecv, ysend, yrecv, gw,
-    lsem, ssem, agsem, csem, rsem, zsem, ysem,
+    g0, gsend, grecv, f0, fsend, frecv, tsend, trecv, y0, ysend, yrecv, gw,
+    lsem, ssem, agsem, csem, rsem, zsem, fsem, tsem, ysem,
 ):
     row, col = lax.axis_index("row"), lax.axis_index("col")
     core = lax.rem(row, 2)
@@ -174,89 +188,82 @@
             block = g[h * BLK:(h + 1) * BLK]
             if d == 0:
                 g0[...] = block
+            elif d in NEAR:
+                i = NEAR.index(d)
+                gsend[i] = block.astype(BF16)
+                send(gsend.at[i], grecv.at[i], zsem.at[i], at(d=d))
             else:
-                gsend[d] = block.astype(BF16)
-                send(gsend.at[d], grecv.at[d], zsem.at[d], at(d=d))
-
-    def weight_grads():
-        out = []
-        for a, (lhs, rhs, dst) in enumerate(
-            ((hid, act.at[1], gwout_hbm), (act.at[0], pg, gwin_hbm))
-        ):
-            step = 256
-            for i in range(lhs.shape[1] // step):
-                r = pl.ds(i * step, step)
-                gw[a, r] = lax.dot_general(
-                    lhs[:, r], rhs[...], (((0,), (0,)), ((), ())), preferred_element_type=F32
-                ).astype(BF16)
-                c = pltpu.make_async_copy(gw.at[a, r], dst.at[r], lsem.at[4 + a * 3 + i])
-                c.start()
-                out.append(c)
-        return out
-
-    forward(0, 0)
-    for e in (1, 3, 2):
-        send(piece(0, 0), piece(0, e), agsem.at[0, e], at(e=NYH - e))
-    for e in (1, 3):
-        take(0, e)
-    take_ring(1, 0)
-    take(0, 2)
-    for e in (1, 3):
-        take_ring(1, e)
-    take_ring(2, 0)
-    take_ring(1, 2)
-    loads[2].wait()
-    loads[3].wait()
-    multiply(0)
-    for e in (1, 3):
-        take_ring(2, e)
-    scatter(0)
-    take_ring(3, 0)
-    take_ring(2, 2)
-    multiply(1)
-    for e in (1, 3):
-        take_ring(3, e)
-    scatter(1)
-    take_ring(3, 2)
-    multiply(2)
-    activation(0)
-    scatter(2)
-    for e in (0, 1, 3, 2):
-        take(4, e)
-    multiply(3)
-    activation(1)
-    scatter(3)
-    share(0)
-    activation(2)
-    back(0)
-    share(1)
-    activation(3)
-    back(1)
-    share(2)
-    back(2)
-    share(3)
-    back(3)
-    stores = weight_grads()
-    total = g0[...]
-    for d in range(1, NZ):
-        arrived(grecv.at[d], zsem.at[d])
-        total = total + grecv[d].astype(F32)
-    for e in range(NYH):
-        ysend[e] = total[e * TOK:(e + 1) * TOK]
-    for e in range(1, NYH):
-        send(ysend.at[e], yrecv.at[e], ysem.at[e], at(e=e))
-    total = ysend[0]
-    for e in range(1, NYH):
-        arrived(yrecv.at[e], ysem.at[e])
-        total = total + yrecv[e]
-    gi_ref[...] = total.astype(BF16)
+                i = FAR.index(d)
+                f0[i] = block[:TOK]
+                fsend[i] = block[TOK:].astype(BF16).reshape(fsend.shape[1:])
+                for e in range(1, NYH):
+                    send(fsend.at[i, e - 1], frecv.at[i, e - 1], fsem.at[i], at(e=e))
+
+    def far(d):
+        i = FAR.index(d)
+        arrived(frecv.at[i], fsem.at[i])
+        total = f0[i]
+        for e in range(NYH - 1):
+            total = total + frecv[i, e].astype(F32)
+        tsend[i] = total.astype(BF16)
+        send(tsend.at[i], trecv.at[i], tsem.at[i], at(d=d))
+
+    def weight_grads(a):
+        lhs, rhs, dst = ((hid, act.at[1], gwout_hbm), (act.at[0], pg, gwin_hbm))[a]
+        for i in range(lhs.shape[1] // TILE):
+            r = pl.ds(i * TILE, TILE)
+            gw[a, r] = lax.dot_general(
+                lhs[:, r], rhs[...], (((0,), (0,)), ((), ())), preferred_element_type=F32
+            ).astype(BF16)
+            c = pltpu.make_async_copy(gw.at[a, r], dst.at[r], lsem.at[4 + a * 3 + i])
+            c.start()
+            stores.append(c)
+
+    def gather_start():
+        forward(0, 0)
+        for e in (1, 3, 2):
+            send(piece(0, 0), piece(0, e), agsem.at[0, e], at(e=NYH - e))
+
+    def weights_ready():
+        loads[2].wait()
+        loads[3].wait()
+
+    stores = []
+
+    def near():
+        total = g0[...]
+        for i in range(len(NEAR)):
+            arrived(grecv.at[i], zsem.at[i])
+            total = total + grecv[i].astype(F32)
+        y0[...] = total[:TOK]
+        ysend[...] = total[TOK:].astype(BF16).reshape(ysend.shape)
+        for e in range(1, NYH):
+            send(ysend.at[e - 1], yrecv.at[e - 1], ysem.at[0], at(e=e))
+
+    def finish():
+        total = y0[...]
+        arrived(yrecv, ysem.at[0])
+        for e in range(NYH - 1):
+            total = total + yrecv[e].astype(F32)
+        for i in range(len(FAR)):
+            arrived(trecv.at[i], tsem.at[i])
+            total = total + trecv[i].astype(F32)
+        gi_ref[...] = total.astype(BF16)
+
+    steps = {
+        "start": gather_start, "take": take, "ring": take_ring, "weights": weights_ready,
+        "mul": multiply, "scatter": scatter, "act": activation, "share": share, "back": back,
+        "far": far, "grads": weight_grads, "near": near, "end": finish,
+    }
+    for name, *args in ORDER:
+        steps[name](*args)
     for c in sent:
         c.wait_send()
     for c in stores:
         c.wait()
 
 
-N_SENDS = 32 + 3 + 2 * NCH + 2 * 7 * NCH + (NZ - 1) + (NYH - 1)
+N_SENDS = 32 + 3 + 2 * NCH + 2 * 7 * NCH + len(NEAR) + 4 * len(FAR) + (NYH - 1)
 
 
 def local(inputs, w_in, w_out, out_grad):
@@ -287,21 +294,29 @@
             vmem((tokens, ff), BF16),
             vmem((tokens, ff), BF16),
             vmem((BLK, feat), F32),
-            vmem((NZ, BLK, feat), BF16),
-            vmem((NZ, BLK, feat), BF16),
-            vmem((NYH, TOK, feat), F32),
-            vmem((NYH, TOK, feat), F32),
+            vmem((len(NEAR), BLK, feat), BF16),
+            vmem((len(NEAR), BLK, feat), BF16),
+            vmem((len(FAR), TOK, feat), F32),
+            vmem((len(FAR), NYH - 1, TOK, feat), BF16),
+            vmem((len(FAR), NYH - 1, TOK, feat), BF16),
+            vmem((len(FAR), TOK, feat), BF16),
+            vmem((len(FAR), TOK, feat), BF16),
+            vmem((TOK, feat), F32),
+            vmem((NYH - 1, TOK, feat), BF16),
+            vmem((NYH - 1, TOK, feat), BF16),
             vmem((2, feat, ff), BF16),
             pltpu.SemaphoreType.DMA((10,)),
             pltpu.SemaphoreType.DMA((N_SENDS,)),
             pltpu.SemaphoreType.DMA((NZ + 1, NYH)),
             pltpu.SemaphoreType.DMA((2, NCH)),
             pltpu.SemaphoreType.DMA((2, NCH)),
-            pltpu.SemaphoreType.DMA((NZ,)),
-            pltpu.SemaphoreType.DMA((NYH,)),
+            pltpu.SemaphoreType.DMA((len(NEAR),)),
+            pltpu.SemaphoreType.DMA((len(FAR),)),
+            pltpu.SemaphoreType.DMA((len(FAR),)),
+            pltpu.SemaphoreType.DMA((1,)),
         ],
         compiler_params=pltpu.CompilerParams(
-            collective_id=0, has_side_effects=True, vmem_limit_bytes=48 * 2**20
+            collective_id=0, has_side_effects=True, vmem_limit_bytes=56 * 2**20
         ),
         cost_estimate=pl.CostEstimate(
             flops=10 * tokens * feat * ff, bytes_accessed=8 * feat * ff, transcendentals=0

time: 85.1 us -> 73.9 us (0.87)
  Pallas kernels: 77.4 us -> 68.2 us
  local copies, waits for them, and re-layouts: 6.64 us -> 4.82 us
    pallas_call x1, Pallas kernels: 77.4 us -> 68.2 us  [local(): pl.pallas_call(kernel, out_shape=(jax.ShapeDtypeStruct(inputs.shape, BF16...]
    unnamed x11 -> x5, local copies, waits for them, and re-layouts: 6.64 us -> 4.82 us
where the time goes in v2:
time: 73.9 us; the launch traced here: 73.7 us
  Pallas kernels  68.2 us (92%)
  local copies, waits for them, and re-layouts  4.82 us (7%)
    pallas_call x1, Pallas kernels, local(): pl.pallas_call(kernel, out_shape=(jax.ShapeDtypeStruct(inputs.shape, BF16...  68.2 us
    unnamed x5, local copies, waits for them, and re-layouts  4.82 us

profile of v2, /device:TPU:1, one launch (start us, length us, event | category | flops | bytes accessed | tf_op | source)
XLA Modules:
  0.0 73.7 jit_solution(9268330043875233078)
XLA Ops:
  0.6 68.2 %shard_map.67 = (bf16[16,768]{1,0:T(8,128)(2,1)}, bf16[768,768]{1,0:T(8,128)(2,1)}, bf16[768,768]{1,0:T(8,128)(2,1)}) custom-call(bf16[16,768]{1,0:T(8,128)(2,1)} %x_hbm.1, bf16[768,768]{1,0:T(8,128)(2,1)} %win_hbm.1, bf16[768,768]{1,0:T(8,128)(2,1)} %wout_hbm.1, bf16[16,768]{1,0:T(8,128)(2,1)} %og_hbm.1), custom_call_target="tpu_custom_call" | custom-call | flops 3019898880 | bytes 4718592 | tf_op jit(solution)/shard_map/pallas_call | solution.py:275
  68.8 1.3 %copy.10 = bf16[16,768]{1,0:T(8,128)(2,1)} copy(bf16[16,768]{1,0:T(8,128)(2,1)} %get-tuple-element.6) | data formatting | bytes 49152
  70.2 0.0 copy-start
  70.2 2.5 %copy.11 = bf16[768,768]{1,0:T(8,128)(2,1)} copy(bf16[768,768]{1,0:T(8,128)(2,1)} %get-tuple-element.7) | data formatting | bytes 2359296
  72.6 0.0 copy-done
  72.6 1.0 %copy.12 = bf16[768,768]{1,0:T(8,128)(2,1)} copy(bf16[768,768]{1,0:T(8,128)(2,1)S(1)} %copy-done) | data formatting | bytes 2359296
Async XLA Ops:
  70.2 2.5 %copy-start = (bf16[768,768]{1,0:T(8,128)(2,1)S(1)}, bf16[768,768]{1,0:T(8,128)(2,1)}, u32[]{:S(2)}) copy-start(bf16[768,768]{1,0:T(8,128)(2,1)} %get-tuple-element.8) | copy-start | bytes 3538948

commit v3 on v2

--- a/solution.py
+++ b/solution.py
@@ -18,21 +18,21 @@
 CH = 2 * BLK
 NCH = 4
 TILE = 256
-POS = {0: 0, 1: 1, 7: 2, 2: 3, 6: 4, 3: 5, 5: 6, 4: 7}
+POS = {1: 0, 7: 1, 2: 2, 6: 3, 3: 4, 5: 5, 0: 6, 4: 7}
 DIST = {p: d for d, p in POS.items()}
 NEAR, FAR = (1, 7, 2, 6), (3, 5, 4)
-HOPS = [(dx, dy) for dy in range(NYL) for dx in range(NX) if (dx, dy) != (0, 0)]
+YHOPS = [2, 1, 3]
+HOPS = [(2, 1), (2, 0), (1, 1), (3, 1), (1, 0), (3, 0), (0, 1)]
 
 ORDER = [
-    ("start",), ("ring", 1, 0), ("take", 0, 1), ("take", 0, 3), ("ring", 2, 0), ("take", 0, 2),
-    ("ring", 1, 1), ("ring", 1, 3), ("ring", 3, 0), ("ring", 1, 2),
-    ("weights",), ("mul", 0), ("ring", 2, 1), ("ring", 2, 3), ("scatter", 0),
-    ("ring", 2, 2), ("mul", 1), ("ring", 3, 1), ("ring", 3, 3), ("scatter", 1),
-    ("take", 4, 0), ("ring", 3, 2), ("mul", 2), ("act", 0), ("scatter", 2),
-    ("take", 4, 1), ("take", 4, 3), ("take", 4, 2), ("mul", 3), ("act", 1), ("scatter", 3),
-    ("share", 0), ("act", 2), ("back", 0), ("share", 1), ("act", 3), ("back", 1),
-    ("share", 2), ("back", 2), ("share", 3), ("back", 3), ("far", 3), ("grads", 0), ("near",),
-    ("far", 5), ("far", 4), ("grads", 1), ("end",),
+    ("start",), ("ring", 1, 0), ("take", 0, 3), ("take", 0, 1), ("take", 0, 2), ("ring", 1, 3),
+    ("ring", 1, 1), ("ring", 1, 2), ("ring", 2, 0), ("weights",), ("mul", 0), ("ring", 2, 3),
+    ("ring", 2, 1), ("scatter", 0), ("ring", 2, 2), ("mul", 1), ("ring", 3, 3), ("ring", 3, 0),
+    ("scatter", 1), ("ring", 3, 1), ("ring", 3, 2), ("mul", 2), ("act", 0), ("take", 4, 0),
+    ("scatter", 2), ("take", 4, 1), ("take", 4, 2), ("take", 4, 3), ("mul", 3), ("scatter", 3),
+    ("act", 2), ("act", 1), ("share", 0), ("act", 3), ("back", 0), ("share", 2), ("back", 2),
+    ("share", 1), ("share", 3), ("back", 1), ("back", 3), ("far", 3), ("far", 5), ("far", 4),
+    ("near",), ("grads", 1), ("grads", 0), ("end",),
 ]
 
 
@@ -70,9 +70,10 @@
     def chip(dx, dy):
         return lax.rem(ylo + dy, NYL) * NX + lax.rem(x + dx, NX)
 
+    own = pl.ds(POS[0] * BLK, TOK)
     loads = [
-        pltpu.make_async_copy(x_hbm, act.at[0, pl.ds(0, TOK)], lsem.at[0]),
-        pltpu.make_async_copy(og_hbm, act.at[1, pl.ds(0, TOK)], lsem.at[1]),
+        pltpu.make_async_copy(x_hbm, act.at[0, own], lsem.at[0]),
+        pltpu.make_async_copy(og_hbm, act.at[1, own], lsem.at[1]),
         pltpu.make_async_copy(win_hbm, win, lsem.at[2]),
         pltpu.make_async_copy(wout_hbm, wout, lsem.at[3]),
     ]
@@ -196,7 +197,7 @@
                 i = FAR.index(d)
                 f0[i] = block[:TOK]
                 fsend[i] = block[TOK:].astype(BF16).reshape(fsend.shape[1:])
-                for e in range(1, NYH):
+                for e in YHOPS:
                     send(fsend.at[i, e - 1], frecv.at[i, e - 1], fsem.at[i], at(e=e))
 
     def far(d):
@@ -221,8 +222,8 @@
 
     def gather_start():
         forward(0, 0)
-        for e in (1, 3, 2):
-            send(piece(0, 0), piece(0, e), agsem.at[0, e], at(e=NYH - e))
+        for e in YHOPS:
+            send(piece(0, 0), piece(0, e), agsem.at[POS[0], e], at(e=NYH - e))
 
     def weights_ready():
         loads[2].wait()
@@ -237,7 +238,7 @@
             total = total + grecv[i].astype(F32)
         y0[...] = total[:TOK]
         ysend[...] = total[TOK:].astype(BF16).reshape(ysend.shape)
-        for e in range(1, NYH):
+        for e in YHOPS:
             send(ysend.at[e - 1], yrecv.at[e - 1], ysem.at[0], at(e=e))
 
     def finish():
@@ -316,12 +317,12 @@
             pltpu.SemaphoreType.DMA((1,)),
         ],
         compiler_params=pltpu.CompilerParams(
-            collective_id=0, has_side_effects=True, vmem_limit_bytes=56 * 2**20
+            collective_id=0, has_side_effects=True, vmem_limit_bytes=48 * 2**20
         ),
         cost_estimate=pl.CostEstimate(
             flops=10 * tokens * feat * ff, bytes_accessed=8 * feat * ff, transcendentals=0
         ),
-    )(inputs, w_in, w_out, out_grad)
+    )(*(pltpu.with_memory_space_constraint(a, pltpu.HBM) for a in (inputs, w_in, w_out, out_grad)))
 
 
 def solution(mesh):

time: 73.9 us -> 68.3 us (0.924)
  Pallas kernels: 68.2 us -> 64.7 us
  local copies, waits for them, and re-layouts: 4.82 us -> 2.64 us
    pallas_call x1, Pallas kernels: 68.2 us -> 64.7 us  [local(): pl.pallas_call(kernel, out_shape=(jax.ShapeDtypeStruct(inputs.shape, BF16...]
    unnamed x5 -> x3, local copies, waits for them, and re-layouts: 4.82 us -> 2.64 us
where the time goes in v3:
time: 68.3 us; the launch traced here: 68 us
  Pallas kernels  64.7 us (95%)
  local copies, waits for them, and re-layouts  2.64 us (4%)
    pallas_call x1, Pallas kernels, local(): pl.pallas_call(kernel, out_shape=(jax.ShapeDtypeStruct(inputs.shape, BF16...  64.7 us
    unnamed x3, local copies, waits for them, and re-layouts  2.64 us

profile of v3, /device:TPU:1, one launch (start us, length us, event | category | flops | bytes accessed | tf_op | source)
XLA Modules:
  0.0 68.0 jit_solution(1470406491101766244)
XLA Ops:
  0.6 64.7 %shard_map.67 = (bf16[16,768]{1,0:T(8,128)(2,1)S(1)}, bf16[768,768]{1,0:T(8,128)(2,1)S(1)}, bf16[768,768]{1,0:T(8,128)(2,1)S(1)}) custom-call(bf16[16,768]{1,0:T(8,128)(2,1)} %x_hbm.1, bf16[768,768]{1,0:T(8,128)(2,1)} %win_hbm.1, bf16[768,768]{1,0:T(8,128)(2,1)} %wout_hbm.1, bf16[16,768]{1,0:T(8,128)(2,1)} %og_hbm.1), custom_call_target="tpu_custom_call" | custom-call | flops 3019898880 | bytes 4718592 | tf_op jit(solution)/shard_map/pallas_call | solution.py:276
  65.3 0.6 copy.10
  66.0 1.0 %copy.11 = bf16[768,768]{1,0:T(8,128)(2,1)} copy(bf16[768,768]{1,0:T(8,128)(2,1)S(1)} %get-tuple-element.7) | data formatting | bytes 2359296
  67.0 1.0 %copy.12 = bf16[768,768]{1,0:T(8,128)(2,1)} copy(bf16[768,768]{1,0:T(8,128)(2,1)S(1)} %get-tuple-element.8) | data formatting | bytes 2359296

commit v4 on v3

--- a/solution.py
+++ b/solution.py
@@ -32,7 +32,7 @@
     ("scatter", 2), ("take", 4, 1), ("take", 4, 2), ("take", 4, 3), ("mul", 3), ("scatter", 3),
     ("act", 2), ("act", 1), ("share", 0), ("act", 3), ("back", 0), ("share", 2), ("back", 2),
     ("share", 1), ("share", 3), ("back", 1), ("back", 3), ("far", 3), ("far", 5), ("far", 4),
-    ("near",), ("grads", 1), ("grads", 0), ("end",),
+    ("near",), ("grads", 1), ("grads", 0), ("drain",), ("end",),
 ]
 
 
@@ -251,20 +251,34 @@
             total = total + trecv[i].astype(F32)
         gi_ref[...] = total.astype(BF16)
 
+    def drain():
+        for c in sent:
+            c.wait_send()
+        for c in stores:
+            c.wait()
+
     steps = {
         "start": gather_start, "take": take, "ring": take_ring, "weights": weights_ready,
         "mul": multiply, "scatter": scatter, "act": activation, "share": share, "back": back,
-        "far": far, "grads": weight_grads, "near": near, "end": finish,
+        "far": far, "grads": weight_grads, "near": near, "drain": drain, "end": finish,
     }
     for name, *args in ORDER:
         steps[name](*args)
-    for c in sent:
-        c.wait_send()
-    for c in stores:
+
+
+N_SENDS = 32 + 3 + 2 * NCH + 2 * 7 * NCH + len(NEAR) + 4 * len(FAR) + (NYH - 1)
+
+
+def store(*refs):
+    n = len(refs) // 2
+    copies = [
+        pltpu.make_async_copy(src, dst, refs[-1].at[i])
+        for i, (src, dst) in enumerate(zip(refs[:n], refs[n:2 * n]))
+    ]
+    for c in copies:
+        c.start()
+    for c in copies:
         c.wait()
-
-
-N_SENDS = 32 + 3 + 2 * NCH + 2 * 7 * NCH + len(NEAR) + 4 * len(FAR) + (NYH - 1)
 
 
 def local(inputs, w_in, w_out, out_grad):
@@ -273,13 +287,10 @@
     tokens = TOK * NYH * NZ
     any_spec = pl.BlockSpec(memory_space=pl.ANY)
     vmem = pltpu.VMEM
-    return pl.pallas_call(
+    out_shape = tuple(jax.ShapeDtypeStruct(a.shape, BF16) for a in (inputs, w_in, w_out))
+    outs = pl.pallas_call(
         kernel,
-        out_shape=(
-            jax.ShapeDtypeStruct(inputs.shape, BF16),
-            jax.ShapeDtypeStruct(w_in.shape, BF16),
-            jax.ShapeDtypeStruct(w_out.shape, BF16),
-        ),
+        out_shape=out_shape,
         in_specs=[any_spec] * 4,
         out_specs=(pl.BlockSpec(memory_space=pltpu.VMEM), any_spec, any_spec),
         scratch_shapes=[
@@ -323,6 +334,15 @@
             flops=10 * tokens * feat * ff, bytes_accessed=8 * feat * ff, transcendentals=0
         ),
     )(*(pltpu.with_memory_space_constraint(a, pltpu.HBM) for a in (inputs, w_in, w_out, out_grad)))
+    return pl.pallas_call(
+        store,
+        out_shape=out_shape,
+        in_specs=[any_spec] * 3,
+        out_specs=(any_spec,) * 3,
+        scratch_shapes=[pltpu.SemaphoreType.DMA((3,))],
+        compiler_params=pltpu.CompilerParams(vmem_limit_bytes=2**20),
+        cost_estimate=pl.CostEstimate(flops=0, bytes_accessed=8 * feat * ff, transcendentals=0),
+    )(*(pltpu.with_memory_space_constraint(a, pltpu.VMEM) for a in outs))
 
 
 def solution(mesh):

time: 68.3 us -> 66.9 us (0.980)
  local copies, waits for them, and re-layouts: 2.64 us -> 0 us
  Pallas kernels: 64.7 us -> 66 us
    unnamed x3 -> x0, local copies, waits for them, and re-layouts: 2.64 us -> none
    pallas_call x1 -> x2, Pallas kernels: 64.7 us -> 66 us  [the longest x1 64.5 us: local(): pl.pallas_call(kernel, out_shape=out_shape, in_specs=[any_spec] * 4, out_...]
where the time goes in v4:
time: 66.9 us; the launch traced here: 66.6 us
  Pallas kernels  66 us (99%)
    pallas_call x1, Pallas kernels, local(): pl.pallas_call(kernel, out_shape=out_shape, in_specs=[any_spec] * 4, out_...  64.5 us
    pallas_call x1, Pallas kernels, local(): pl.pallas_call(store, out_shape=out_shape, in_specs=[any_spec] * 3, out_s...  1.44 us

profile of v4, /device:TPU:1, one launch (start us, length us, event | category | flops | bytes accessed | tf_op | source)
XLA Modules:
  0.0 66.6 jit_solution(15558696047498624296)
XLA Ops:
  0.6 64.5 %shard_map.67 = (bf16[16,768]{1,0:T(8,128)(2,1)S(1)}, bf16[768,768]{1,0:T(8,128)(2,1)S(1)}, bf16[768,768]{1,0:T(8,128)(2,1)S(1)}) custom-call(bf16[16,768]{1,0:T(8,128)(2,1)} %x_hbm.1, bf16[768,768]{1,0:T(8,128)(2,1)} %win_hbm.1, bf16[768,768]{1,0:T(8,128)(2,1)} %wout_hbm.1, bf16[16,768]{1,0:T(8,128)(2,1)} %og_hbm.1), custom_call_target="tpu_custom_call" | custom-call | flops 3019898880 | bytes 4718592 | tf_op jit(solution)/shard_map/pallas_call | solution.py:291
  65.2 1.4 %shard_map.68 = (bf16[16,768]{1,0:T(8,128)(2,1)}, bf16[768,768]{1,0:T(8,128)(2,1)}, bf16[768,768]{1,0:T(8,128)(2,1)}) custom-call(bf16[16,768]{1,0:T(8,128)(2,1)S(1)} %get-tuple-element.6.refs_0_, bf16[768,768]{1,0:T(8,128)(2,1)S(1)} %get-tuple-element.7.refs_1_, bf16[768,768]{1,0:T(8,128)(2,1)S(1)} %get-tuple-element.8.refs_2_), custom_call_target="tpu_custom_call" | custom-call | bytes 4718592 | tf_op jit(solution)/shard_map/pallas_call | solution.py:337

commit v5 on v4

--- a/solution.py
+++ b/solution.py
@@ -83,7 +83,7 @@
         [at(dc=1)]
         + [at(dx=dx, dy=dy) for dx, dy in HOPS]
         + [at(e=e) for e in range(1, NYH)]
-        + [at(d=d) for d in range(1, NZ)]
+        + [at(d=d) for d in (1, NZ - 1)]
     )
     barrier = pltpu.get_barrier_semaphore()
     for p in peers:

time: 66.9 us -> 67.4 us (level)
  no operation moved by 1% of the time
where the time goes in v5:
time: 67.4 us; the launch traced here: 67.2 us
  Pallas kernels  66.6 us (99%)
    pallas_call x1, Pallas kernels, local(): pl.pallas_call(kernel, out_shape=out_shape, in_specs=[any_spec] * 4, out_...  65.2 us
    pallas_call x1, Pallas kernels, local(): pl.pallas_call(store, out_shape=out_shape, in_specs=[any_spec] * 3, out_s...  1.44 us

profile of v5, /device:TPU:1, one launch (start us, length us, event | category | flops | bytes accessed | tf_op | source)
XLA Modules:
  0.0 67.2 jit_solution(13988830885802529490)
XLA Ops:
  0.6 65.2 %shard_map.67 = (bf16[16,768]{1,0:T(8,128)(2,1)S(1)}, bf16[768,768]{1,0:T(8,128)(2,1)S(1)}, bf16[768,768]{1,0:T(8,128)(2,1)S(1)}) custom-call(bf16[16,768]{1,0:T(8,128)(2,1)} %x_hbm.1, bf16[768,768]{1,0:T(8,128)(2,1)} %win_hbm.1, bf16[768,768]{1,0:T(8,128)(2,1)} %wout_hbm.1, bf16[16,768]{1,0:T(8,128)(2,1)} %og_hbm.1), custom_call_target="tpu_custom_call" | custom-call | flops 3019898880 | bytes 4718592 | tf_op jit(solution)/shard_map/pallas_call | solution.py:291
  65.8 1.4 %shard_map.68 = (bf16[16,768]{1,0:T(8,128)(2,1)}, bf16[768,768]{1,0:T(8,128)(2,1)}, bf16[768,768]{1,0:T(8,128)(2,1)}) custom-call(bf16[16,768]{1,0:T(8,128)(2,1)S(1)} %get-tuple-element.6.refs_0_, bf16[768,768]{1,0:T(8,128)(2,1)S(1)} %get-tuple-element.7.refs_1_, bf16[768,768]{1,0:T(8,128)(2,1)S(1)} %get-tuple-element.8.refs_2_), custom_call_target="tpu_custom_call" | custom-call | bytes 4718592 | tf_op jit(solution)/shard_map/pallas_call | solution.py:337

commit v6 on v4

--- a/solution.py
+++ b/solution.py
@@ -25,8 +25,8 @@
 HOPS = [(2, 1), (2, 0), (1, 1), (3, 1), (1, 0), (3, 0), (0, 1)]
 
 ORDER = [
-    ("start",), ("ring", 1, 0), ("take", 0, 3), ("take", 0, 1), ("take", 0, 2), ("ring", 1, 3),
-    ("ring", 1, 1), ("ring", 1, 2), ("ring", 2, 0), ("weights",), ("mul", 0), ("ring", 2, 3),
+    ("start",), ("weights",), ("ring", 1, 0), ("take", 0, 3), ("take", 0, 1), ("take", 0, 2), ("ring", 1, 3),
+    ("ring", 1, 1), ("ring", 1, 2), ("ring", 2, 0), ("mul", 0), ("ring", 2, 3),
     ("ring", 2, 1), ("scatter", 0), ("ring", 2, 2), ("mul", 1), ("ring", 3, 3), ("ring", 3, 0),
     ("scatter", 1), ("ring", 3, 1), ("ring", 3, 2), ("mul", 2), ("act", 0), ("take", 4, 0),
     ("scatter", 2), ("take", 4, 1), ("take", 4, 2), ("take", 4, 3), ("mul", 3), ("scatter", 3),
@@ -49,7 +49,7 @@
 def kernel(
     x_hbm, win_hbm, wout_hbm, og_hbm,
     gi_ref, gwin_hbm, gwout_hbm,
-    act, win, wout, part, crecv, sendb, own32, rrecv, agall, hid, pg,
+    act, win, wout, win_t, wout_t, part, crecv, sendb, own32, rrecv, agall, hid, pg,
     g0, gsend, grecv, f0, fsend, frecv, tsend, trecv, y0, ysend, yrecv, gw,
     lsem, ssem, agsem, csem, rsem, zsem, fsem, tsem, ysem,
 ):
@@ -141,9 +141,7 @@
         pre = jnp.dot(act[0, rows], win[...], preferred_element_type=F32)
         part[ci, 0, 0] = pre[:BLK]
         part[ci, 1, 0] = pre[BLK:]
-        hg = lax.dot_general(
-            act[1, rows], wout[...], (((1,), (1,)), ((), ())), preferred_element_type=F32
-        )
+        hg = jnp.dot(act[1, rows], wout_t[...], preferred_element_type=F32)
         part[ci, 0, 1] = hg[:BLK]
         part[ci, 1, 1] = hg[BLK:]
         send(part.at[ci, 1 - core], crecv.at[ci], csem.at[0, ci], at(dc=1))
@@ -181,9 +179,7 @@
                 c = pl.ds((k // NX) * half, half)
                 hid[r, c] = agall[ci, h, k, 0]
                 pg[r, c] = agall[ci, h, k, 1]
-        g = lax.dot_general(
-            pg[pl.ds(ci * CH, CH)], win[...], (((1,), (1,)), ((), ())), preferred_element_type=F32
-        )
+        g = jnp.dot(pg[pl.ds(ci * CH, CH)], win_t[...], preferred_element_type=F32)
         for h in range(2):
             d = DIST[2 * ci + h]
             block = g[h * BLK:(h + 1) * BLK]
@@ -227,7 +223,9 @@
 
     def weights_ready():
         loads[2].wait()
+        win_t[...] = win[...].T
         loads[3].wait()
+        wout_t[...] = wout[...].T
 
     stores = []
 
@@ -297,6 +295,8 @@
             vmem((2, tokens, feat), BF16),
             vmem((feat, ff), BF16),
             vmem((ff, feat), BF16),
+            vmem((ff, feat), BF16),
+            vmem((feat, ff), BF16),
             vmem((NCH, 2, 2, BLK, ff), F32),
             vmem((NCH, 2, BLK, ff), F32),
             vmem((NCH, NQ, 2, TOK, half), BF16),

time: 66.9 us -> 67.1 us (level)
  no operation moved by 1% of the time
where the time goes in v6:
time: 67.1 us; the launch traced here: 66.6 us
  Pallas kernels  65.9 us (98%)
    pallas_call x1, Pallas kernels, local(): pl.pallas_call(kernel, out_shape=out_shape, in_specs=[any_spec] * 4, out_...  64.5 us
    pallas_call x1, Pallas kernels, local(): pl.pallas_call(store, out_shape=out_shape, in_specs=[any_spec] * 3, out_s...  1.44 us

profile of v6, /device:TPU:1, one launch (start us, length us, event | category | flops | bytes accessed | tf_op | source)
XLA Modules:
  0.0 66.6 jit_solution(14283410949452434084)
XLA Ops:
  0.6 64.5 %shard_map.67 = (bf16[16,768]{1,0:T(8,128)(2,1)S(1)}, bf16[768,768]{1,0:T(8,128)(2,1)S(1)}, bf16[768,768]{1,0:T(8,128)(2,1)S(1)}) custom-call(bf16[16,768]{1,0:T(8,128)(2,1)} %x_hbm.1, bf16[768,768]{1,0:T(8,128)(2,1)} %win_hbm.1, bf16[768,768]{1,0:T(8,128)(2,1)} %wout_hbm.1, bf16[16,768]{1,0:T(8,128)(2,1)} %og_hbm.1), custom_call_target="tpu_custom_call" | custom-call | flops 3019898880 | bytes 4718592 | tf_op jit(solution)/shard_map/pallas_call | solution.py:289
  65.1 1.4 %shard_map.68 = (bf16[16,768]{1,0:T(8,128)(2,1)}, bf16[768,768]{1,0:T(8,128)(2,1)}, bf16[768,768]{1,0:T(8,128)(2,1)}) custom-call(bf16[16,768]{1,0:T(8,128)(2,1)S(1)} %get-tuple-element.6.refs_0_, bf16[768,768]{1,0:T(8,128)(2,1)S(1)} %get-tuple-element.7.refs_1_, bf16[768,768]{1,0:T(8,128)(2,1)S(1)} %get-tuple-element.8.refs_2_), custom_call_target="tpu_custom_call" | custom-call | bytes 4718592 | tf_op jit(solution)/shard_map/pallas_call | solution.py:337
